TPU v7x, 32 devices: a whole 2x2x4 slice. The times are simulated.
32 devices in a mesh: band: 16 (over z, y, x), strip: 2 (over core).
Axes of the slice: x: 2, y: 2, z: 4, core: 2. Of those that a mesh axis runs over, the one named last changes fastest.
Arguments:
- coeffs: bfloat16 [128, 128, 2048], P('strip', None, 'band'), may hold values from -4.1875 to 4.1875
- hamiltonian: bfloat16 [128, 5, 128, 128], P('strip'), may hold values from -0.15625 to 0.15625
- adjacency: int32 [128, 5], P('strip'), may hold values from 0 to 127, as said below
- occupation: float32 [2048], P('band'), may hold values from 0.1 to 2
Outputs:
- density: float32 [128, 128, 128], P(('strip', 'band'))
Inputs may be any that keep to these rules, and one draw needn't show every extreme that they name: `adjacency`: row e lists element e itself and its four neighbours on the periodic 8 x 16 sheet of elements, numbered row * 16 + column, in an order drawn for each element.
All inputs are finite; a program needn't handle non-finite values.
Results may differ from a plain program's by a relative error of at most 0.019.
Values may be sent and summed in bfloat16 or wider, within the bound.
A program may use at most 128 MiB of HBM per device.

v0:
```python
import jax
import jax.numpy as jnp
from jax import lax
from jax.sharding import PartitionSpec as P

EY = 16
EXS = 4


def with_halo(block, sides, width):
    for axis, dim in sides:
        count = lax.axis_size(axis)
        forward = [(i, i + 1) for i in range(count - 1)]
        forward.append((count - 1, 0))
        backward = [(target, source) for source, target in forward]
        low = lax.ppermute(
            lax.slice_in_dim(block, block.shape[dim] - width, None, axis=dim), axis, forward
        )
        high = lax.ppermute(lax.slice_in_dim(block, 0, width, axis=dim), axis, backward)
        block = jnp.concatenate([low, block, high], axis=dim)
    return block


def apply_operator(field_block, hamiltonian, local_index):
    basis = field_block.shape[1]
    columns = field_block.shape[2]
    blocked = field_block.reshape(EXS, EY, basis, columns)
    padded = with_halo(blocked, (("strip", 0),), 1)
    padded = padded.reshape((EXS + 2) * EY, basis, columns)
    picked = jnp.take(padded, local_index, axis=0)
    return jnp.einsum("ejik,ejkb->eib", hamiltonian, picked, preferred_element_type=jnp.float32)


def local(coeffs, hamiltonian, adjacency, occupation):
    strip_index = lax.axis_index("strip")
    ex_total = EXS * lax.axis_size("strip")
    band_count = lax.axis_size("band")
    rel_row = (adjacency // EY - strip_index * EXS + 1) % ex_total
    local_index = rel_row * EY + adjacency % EY
    degree_one = apply_operator(coeffs, hamiltonian, local_index).astype(jnp.bfloat16)
    degree_two = (
        2.0 * apply_operator(degree_one, hamiltonian, local_index) - coeffs.astype(jnp.float32)
    ).astype(jnp.bfloat16)
    filtered = (
        2.0 * apply_operator(degree_two, hamiltonian, local_index) - degree_one.astype(jnp.float32)
    ).astype(jnp.bfloat16)
    elem_count = filtered.shape[0]
    basis = filtered.shape[1]
    local_bands = filtered.shape[2]
    total_bands = local_bands * band_count
    owned_count = elem_count // band_count
    occ_full = lax.all_gather(occupation, "band", axis=0, tiled=True)
    grouped = filtered.reshape(band_count, owned_count, basis, local_bands)
    item_block = lax.all_to_all(grouped, "band", split_axis=0, concat_axis=3, tiled=True)
    scaled = (item_block.astype(jnp.float32) * occ_full).astype(jnp.bfloat16)
    summed = jnp.einsum("zmib,zmjb->mij", scaled, item_block, preferred_element_type=jnp.float32)
    return summed / total_bands


def solution(mesh):
    return jax.shard_map(
        local,
        mesh=mesh,
        in_specs=(
            P("strip", None, "band"),
            P("strip", None, None, None),
            P("strip", None),
            P("band"),
        ),
        out_specs=P(("strip", "band"), None, None),
        check_vma=False,
    )
```

profile of v0, /device:TPU:0, one launch (start us, length us, event | category | flops | bytes accessed | tf_op | source)
XLA Modules:
  0.0 180.7 jit_solution(13640399663994621651)
XLA Ops:
  0.0 1.3 slice_bitcast_fusion.5
  1.3 0.5 collective-permute-start
  1.8 0.1 collective-permute-start.1
  1.9 0.7 compare_and_fusion
  2.6 0.1 copy.22
  2.7 0.1 reshape.83
  2.8 0.1 copy.19
  2.9 0.4 collective-permute-done
  3.3 0.0 copy-start.2
  3.3 0.7 collective-permute-done.1
  4.1 0.1 copy-done.2
  4.1 0.0 copy-start.3
  4.1 0.8 copy-done.3
  4.9 2.2 %pad_maximum_fusion = bf16[6,16,128,128]{3,2,1,0:T(8,128)(2,1)S(1)} fusion(bf16[1,16,128,128]{3,2,1,0:T(8,128)(2,1)} %copy-done.3, bf16[4,16,128,128]{3,2,1,0:T(8,128)(2,1)} %bitcast.61, bf16[1,16,128,128]{3,2,1,0:T(8,128)(2,1)} %copy-done.2), kind=kLoop, calls=%fused_computation.24 | loop fusion | flops 3145728 | bytes 6291456 | tf_op jit(solution)/shard_map/concatenate | solution.py:20
  7.1 10.7 %gather_fusion = bf16[320,128,128]{2,1,0:T(8,128)(2,1)} fusion(bf16[96,128,128]{2,1,0:T(8,128)(2,1)S(1)} %bitcast.58, s32[1024]{0:T(1024)S(1)} %pad_clamp_fusion), kind=kCustom, calls=%fused_computation.clone | custom fusion | bytes 20972800 | tf_op jit(solution)/shard_map/jit(_take)/gather | solution.py:30
  17.9 14.5 %copy.23 = bf16[64,5,128,128]{2,3,1,0:T(8,128)(2,1)} copy(bf16[64,5,128,128]{3,2,1,0:T(8,128)(2,1)} %bitcast.60) | data formatting | bytes 20971520 | tf_op jit(solution)/shard_map/jit(_take)/gather | solution.py:30
  32.4 0.0 copy-start
  32.4 9.1 %bitcast_convert_fusion = bf16[64,128,128]{2,1,0:T(8,128)(2,1)S(1)} fusion(bf16[64,5,128,128]{3,2,1,0:T(8,128)(2,1)} %param.7, bf16[64,5,128,128]{2,3,1,0:T(8,128)(2,1)} %copy.23, pred[64,5]{1,0:T(8,128)(4,1)S(1)} %copy.19), kind=kOutput, calls=%fused_computation.21 | convolution fusion | flops 1348468736 | bytes 23068992 | tf_op jit(solution)/shard_map/ejik,ejkb->eib/dot_general | solution.py:31
  41.5 0.0 copy-start.1
  41.5 1.3 copy-done.1
  42.8 1.0 slice_bitcast_fusion.3
  43.9 0.4 collective-permute-start.2
  44.3 0.1 collective-permute-start.3
  44.4 0.0 copy-done
  44.4 3.0 %copy.25 = bf16[64,128,128]{1,2,0:T(8,128)(2,1)} copy(bf16[64,128,128]{2,1,0:T(8,128)(2,1)S(1)} %copy-done) | data formatting | bytes 4194304 | tf_op args[0]
  47.4 0.0 collective-permute-done.2
  47.4 0.0 copy-start.4
  47.4 0.0 collective-permute-done.3
  47.4 0.8 copy-done.4
  48.2 0.0 copy-start.5
  48.2 0.8 copy-done.5
  49.0 2.2 %pad_maximum_fusion.1 = bf16[6,16,128,128]{2,3,1,0:T(8,128)(2,1)S(1)} fusion(bf16[1,16,128,128]{2,3,1,0:T(8,128)(2,1)} %copy-done.5, bf16[4,16,128,128]{2,3,1,0:T(8,128)(2,1)} %bitcast.66, bf16[1,16,128,128]{2,3,1,0:T(8,128)(2,1)} %copy-done.4), kind=kLoop, calls=%fused_computation.25 | loop fusion | flops 3145728 | bytes 6291456 | tf_op jit(solution)/shard_map/concatenate | solution.py:20
  51.2 10.7 %gather_fusion.1 = bf16[320,128,128]{1,2,0:T(8,128)(2,1)} fusion(bf16[96,128,128]{1,2,0:T(8,128)(2,1)S(1)} %bitcast.59, s32[1024]{0:T(1024)S(1)} %pad_clamp_fusion), kind=kCustom, calls=%fused_computation.1.clone | custom fusion | bytes 20972800 | tf_op jit(solution)/shard_map/jit(_take)/gather | solution.py:30
  61.9 9.5 %fusion.13 = bf16[64,128,128]{1,2,0:T(8,128)(2,1)S(1)} fusion(bf16[64,128,128]{1,2,0:T(8,128)(2,1)} %copy.25, bf16[64,5,128,128]{3,2,1,0:T(8,128)(2,1)} %param.7, bf16[64,5,128,128]{2,3,1,0:T(8,128)(2,1)} %bitcast.63, pred[64,5]{1,0:T(8,128)(4,1)S(1)} %copy.19), kind=kOutput, calls=%fused_computation.19 | convolution fusion | flops 1351614464 | bytes 25166144 | tf_op jit(solution)/shard_map/ejik,ejkb->eib/dot_general | solution.py:31
  71.4 0.1 slice_bitcast_fusion.1
  71.5 0.4 collective-permute-start.4
  72.0 0.1 collective-permute-start.5
  72.1 1.4 collective-permute-done.4
  73.5 0.7 collective-permute-done.5
  74.3 0.4 pad_maximum_fusion.2
  74.6 10.9 %gather_fusion.2 = bf16[320,128,128]{1,2,0:T(8,128)(2,1)} fusion(bf16[96,128,128]{1,2,0:T(8,128)(2,1)S(1)} %bitcast.57, s32[1024]{0:T(1024)S(1)} %pad_clamp_fusion), kind=kCustom, calls=%fused_computation.2.clone | custom fusion | bytes 20972800 | tf_op jit(solution)/shard_map/jit(_take)/gather | solution.py:30
  85.6 10.8 %fusion.12 = bf16[64,128,128]{1,2,0:T(8,128)(2,1)} fusion(bf16[64,5,128,128]{3,2,1,0:T(8,128)(2,1)} %param.7, bf16[64,5,128,128]{2,3,1,0:T(8,128)(2,1)} %bitcast.62, pred[64,5]{1,0:T(8,128)(4,1)S(1)} %copy.19, bf16[64,128,128]{2,1,0:T(8,128)(2,1)} %copy-done.1), kind=kOutput, calls=%fused_computation.16 | convolution fusion | flops 1351614464 | bytes 25166144 | tf_op jit(solution)/shard_map/ejik,ejkb->eib/dot_general | solution.py:31
  96.4 0.0 copy-start.6
  96.4 8.4 %all-to-all-start = ((bf16[16,4,128,128]{2,3,1,0:T(8,128)(2,1)}), bf16[16,4,128,128]{2,3,1,0:T(8,128)(2,1)S(1)}, u32[]{:S(2)}, u32[]{:S(2)}) async-start(bf16[16,4,128,128]{2,3,1,0:T(8,128)(2,1)} %bitcast.68), calls=%async_computation | async-start | bytes 4194304 | tf_op jit(solution)/shard_map/all_to_all | solution.py:54
  104.8 0.0 copy-done.6
  104.8 68.7 %all-gather = f32[16,1,128]{2,1,0:T(1,128)S(1)} all-gather(f32[1,1,128]{2,1,0:T(1,128)S(1)} %bitcast.70), channel_id=1, replica_groups=mesh['band'=16,'strip'=2] {'band'}, dimensions={0}, use_global_device_ids=true | all-gather | bytes 8704 | tf_op jit(solution)/shard_map/all_gather | solution.py:52
  173.5 0.0 all-to-all-done
  173.5 2.9 %copy.27 = bf16[1,4,128,16,128]{4,3,2,1,0:T(8,128)(2,1)} copy(bf16[1,4,128,16,128]{2,4,1,3,0:T(8,128)(2,1)S(1)} %bitcast.64) | data formatting | bytes 4194304 | tf_op jit(solution)/shard_map/all_to_all | solution.py:54
  176.4 2.8 %all_to_all.16 = bf16[4,128,2048]{2,1,0:T(8,128)(2,1)S(1)} reshape(bf16[1,4,128,16,128]{4,3,2,1,0:T(8,128)(2,1)} %copy.27) | data formatting | bytes 4194304 | tf_op jit(solution)/shard_map/all_to_all | solution.py:54
  179.2 1.4 fusion.22
  (1 shorter events, 0.0 us)
Async XLA Ops:
  1.3 2.1 %collective-permute-start = (bf16[1,16,128,128]{3,2,1,0:T(8,128)(2,1)S(1)}, bf16[1,16,128,128]{3,2,1,0:T(8,128)(2,1)S(1)}, u32[]{:S(2)}, u32[]{:S(2)}) collective-permute-start(bf16[1,16,128,128]{3,2,1,0:T(8,128)(2,1)S(1)} %get-tuple-element.12), channel_id=1, source_target_pairs={{0,1},{1,0},{2,3},{3,2},{4,5},{5,4},{6,7},{7,6},{8,9},{9,8},{10,11... | collective-permute-start | bytes 1572872 | tf_op jit(solution)/shard_map/ppermute | solution.py:16
  1.8 2.3 %collective-permute-start.1 = (bf16[1,16,128,128]{3,2,1,0:T(8,128)(2,1)S(1)}, bf16[1,16,128,128]{3,2,1,0:T(8,128)(2,1)S(1)}, u32[]{:S(2)}, u32[]{:S(2)}) collective-permute-start(bf16[1,16,128,128]{3,2,1,0:T(8,128)(2,1)S(1)} %get-tuple-element.13), channel_id=1, source_target_pairs={{1,0},{0,1},{3,2},{2,3},{5,4},{4,5},{7,6},{6,7},{9,8},{8,9},{11,10... | collective-permute-start | bytes 1572872 | tf_op jit(solution)/shard_map/ppermute | solution.py:19
  3.3 0.8 copy-start.2
  4.1 0.8 copy-start.3
  32.4 12.0 %copy-start = (bf16[64,128,128]{2,1,0:T(8,128)(2,1)S(1)}, bf16[64,128,128]{2,1,0:T(8,128)(2,1)}, u32[]{:S(2)}) copy-start(bf16[64,128,128]{2,1,0:T(8,128)(2,1)} %param.6) | copy-start | bytes 6291460
  41.5 1.3 copy-start.1
  43.9 3.5 %collective-permute-start.2 = (bf16[1,16,128,128]{2,3,1,0:T(8,128)(2,1)}, bf16[1,16,128,128]{2,3,1,0:T(8,128)(2,1)S(1)}, u32[]{:S(2)}, u32[]{:S(2)}) collective-permute-start(bf16[1,16,128,128]{2,3,1,0:T(8,128)(2,1)} %get-tuple-element.10), channel_id=1, source_target_pairs={{0,1},{1,0},{2,3},{3,2},{4,5},{5,4},{6,7},{7,6},{8,9},{9,8},{10,11... | collective-permute-start | bytes 1572872 | tf_op jit(solution)/shard_map/ppermute | solution.py:16
  44.3 3.1 %collective-permute-start.3 = (bf16[1,16,128,128]{2,3,1,0:T(8,128)(2,1)}, bf16[1,16,128,128]{2,3,1,0:T(8,128)(2,1)S(1)}, u32[]{:S(2)}, u32[]{:S(2)}) collective-permute-start(bf16[1,16,128,128]{2,3,1,0:T(8,128)(2,1)} %get-tuple-element.11), channel_id=1, source_target_pairs={{1,0},{0,1},{3,2},{2,3},{5,4},{4,5},{7,6},{6,7},{9,8},{8,9},{11,10... | collective-permute-start | bytes 1572872 | tf_op jit(solution)/shard_map/ppermute | solution.py:19
  47.4 0.8 copy-start.4
  48.2 0.8 copy-start.5
  71.5 2.0 %collective-permute-start.4 = (bf16[1,16,128,128]{2,3,1,0:T(8,128)(2,1)S(1)}, bf16[1,16,128,128]{2,3,1,0:T(8,128)(2,1)S(1)}, u32[]{:S(2)}, u32[]{:S(2)}) collective-permute-start(bf16[1,16,128,128]{2,3,1,0:T(8,128)(2,1)S(1)} %get-tuple-element.8), channel_id=1, source_target_pairs={{0,1},{1,0},{2,3},{3,2},{4,5},{5,4},{6,7},{7,6},{8,9},{9,8},{10,11... | collective-permute-start | bytes 1572872 | tf_op jit(solution)/shard_map/ppermute | solution.py:16
  72.0 2.3 %collective-permute-start.5 = (bf16[1,16,128,128]{2,3,1,0:T(8,128)(2,1)S(1)}, bf16[1,16,128,128]{2,3,1,0:T(8,128)(2,1)S(1)}, u32[]{:S(2)}, u32[]{:S(2)}) collective-permute-start(bf16[1,16,128,128]{2,3,1,0:T(8,128)(2,1)S(1)} %get-tuple-element.9), channel_id=1, source_target_pairs={{1,0},{0,1},{3,2},{2,3},{5,4},{4,5},{7,6},{6,7},{9,8},{8,9},{11,10... | collective-permute-start | bytes 1572872 | tf_op jit(solution)/shard_map/ppermute | solution.py:19
  96.4 8.4 %copy-start.6 = (f32[128]{0:T(128)S(1)}, f32[128]{0:T(128)}, u32[]{:S(2)}) copy-start(f32[128]{0:T(128)} %param.9) | copy-start | bytes 1540
  96.4 77.1 %all-to-all-start = ((bf16[16,4,128,128]{2,3,1,0:T(8,128)(2,1)}), bf16[16,4,128,128]{2,3,1,0:T(8,128)(2,1)S(1)}, u32[]{:S(2)}, u32[]{:S(2)}) async-start(bf16[16,4,128,128]{2,3,1,0:T(8,128)(2,1)} %bitcast.68), calls=%async_computation | async-start | bytes 4194304 | tf_op jit(solution)/shard_map/all_to_all | solution.py:54
where the time goes:
time: 183 us; the launch traced here: 181 us
  blocking collectives  68.7 us (38%)
  local copies, waits for them, and re-layouts  62.1 us (34%)
  matrix products  30.9 us (17%)
  starting transfers between devices  10 us (5%)
  other arithmetic  5.5 us (3%)
  waiting for transfers between devices  3.29 us (2%)
    all_gather x1, blocking collectives, local(): occ_full = lax.all_gather(occupation, 'band', axis=0, tiled=True)  68.7 us
    gather x4, local copies, waits for them, and re-layouts, apply_operator(): picked = jnp.take(padded, local_index, axis=0)  46.9 us
    dot_general x3, matrix products, apply_operator(): jnp.einsum('ejik,ejkb->eib', hamiltonian, picked, preferred_element_type=...  29.5 us
    all_to_all x1, starting transfers between devices, local(): lax.all_to_all(grouped, 'band', split_axis=0, concat_axis=3, tiled=True)  8.36 us
    unnamed x15, local copies, waits for them, and re-layouts  6.76 us
    all_to_all x2, local copies, waits for them, and re-layouts, local(): lax.all_to_all(grouped, 'band', split_axis=0, concat_axis=3, tiled=True)  5.74 us
    concatenate x3, other arithmetic, with_halo(): block = jnp.concatenate([low, block, high], axis=dim)  4.78 us
  transfers between devices with their start and end apart: 7, of which 4 were waited for; matrix products, arithmetic and copies ran while one was open for 2% of the time, Pallas kernels for 0%

commit v1 on v0

v1 whole, which is shorter than its diff:
```python
import functools
import jax
import jax.numpy as jnp
from jax import lax
from jax.experimental import pallas as pl
from jax.experimental.pallas import tpu as pltpu
from jax.sharding import PartitionSpec as P

EY = 16
PAD = 16
MIB = 1 << 20


def lanes(shape):
    return lax.broadcasted_iota(jnp.int32, shape, 1)


def rows(shape):
    return lax.broadcasted_iota(jnp.int32, shape, 0)


def pack_pair(first, second):
    half = first.shape[0] // 2
    left = lanes((half, 2 * half)) < half
    lane = jnp.where(left, lanes(left.shape), lanes(left.shape) - half)
    row = rows(left.shape)
    blocks_1 = jnp.where(left, first[:half], first[half:])
    blocks_2 = jnp.where(left, second[:half], second[half:])
    triangles = jnp.where(row >= lane, blocks_1, blocks_2)
    corners = jnp.where(left, second[half:], first[:half])
    diagonal = jnp.sum(jnp.where(row == lane, blocks_2, 0.0), axis=0, keepdims=True)
    return jnp.concatenate(
        [triangles, corners, jnp.broadcast_to(diagonal, (PAD, 2 * half))], axis=0
    )


def unpack_pair(packed):
    nb = packed.shape[1]
    half = nb // 2
    triangles, corners, diagonal = packed[:half], packed[half:nb], packed[nb:nb + 1]
    left = lanes((half, nb)) < half
    i, j = rows((nb, nb)), lanes((nb, nb))
    same = (i < half) == (j < half)
    wide_1 = jnp.concatenate([jnp.where(left, triangles, corners), triangles], axis=0)
    held_1 = (same & (i >= j)) | ((i < half) & (j >= half))
    first = jnp.where(held_1, wide_1, wide_1.T)
    wide_2 = jnp.concatenate([triangles, jnp.where(left, corners, triangles)], axis=0)
    held_2 = (same & (i < j)) | ((i >= half) & (j < half))
    second = jnp.where(held_2, wide_2, wide_2.T)
    second = jnp.where(i == j, jnp.broadcast_to(diagonal, (nb, nb)), second)
    return first, second


def kernel(
    strips, bands, total_bands,
    adj_ref, occ_ref, coeffs_hbm, ham_hbm, out_ref,
    ham, v0, v1, v2, packed, arrived, crossed, slots,
    ham_sem, v0_sem, halo_send, halo_recv, part_send, part_recv, cross_send, cross_recv,
):
    elems = coeffs_hbm.shape[0]
    row_count = elems // EY
    group = bands // row_count
    bits = group.bit_length() - 1
    owned = EY // group
    pairs = owned // 2
    strip = lax.axis_index("strip")
    band = lax.axis_index("band")
    my_row, mine = band // group, band % group
    above, below = (strip + strips - 1) % strips, (strip + 1) % strips

    def partner(bit):
        step = 1 << bit
        return band + step * (1 - 2 * ((band // step) % 2))

    own_copy = pltpu.make_async_copy(coeffs_hbm, v0.at[pl.ds(EY, elems)], v0_sem)
    own_copy.start()
    per_row = EY * 5
    ham_copies = [
        pltpu.make_async_copy(
            ham_hbm.at[pl.ds(r * per_row, per_row)], ham.at[pl.ds(r * per_row, per_row)], ham_sem.at[r]
        )
        for r in range(row_count)
    ]
    row_order = [1, 0] + [row_count - 1] + list(range(2, row_count - 1))
    for r in row_order:
        ham_copies[r].start()

    barrier = pltpu.get_barrier_semaphore()
    greeted = 0
    for target in [above] if strips == 2 else [above, below]:
        pl.semaphore_signal(barrier, inc=1, device_id={"strip": target})
        greeted += 1
    for bit in range(bits):
        pl.semaphore_signal(barrier, inc=1, device_id={"band": partner(bit)})
        greeted += 1
    for away in range(1, row_count):
        pl.semaphore_signal(
            barrier, inc=1, device_id={"band": ((my_row + away) % row_count) * group + mine}
        )
        greeted += 1
    pl.semaphore_wait(barrier, greeted)

    def halo(field, ref, source, shift):
        up = pltpu.make_async_remote_copy(
            source.at[pl.ds(shift, EY)], ref.at[pl.ds(EY + elems, EY)],
            halo_send.at[2 * field], halo_recv.at[2 * field], device_id={"strip": above},
        )
        down = pltpu.make_async_remote_copy(
            source.at[pl.ds(shift + elems - EY, EY)], ref.at[pl.ds(0, EY)],
            halo_send.at[2 * field + 1], halo_recv.at[2 * field + 1], device_id={"strip": below},
        )
        return up, down

    halos = [halo(0, v0, coeffs_hbm, 0), halo(1, v1, v1, EY), halo(2, v2, v2, EY)]
    for copy in halos[0]:
        copy.start()

    def product(blocks, fields):
        return jnp.dot(
            jnp.concatenate(blocks, axis=1), jnp.concatenate(fields, axis=0),
            preferred_element_type=jnp.float32,
        )

    sheet_rows = row_count * strips

    def first_element(r, c):
        e = r * EY + c
        places = []
        for j in range(5):
            a = adj_ref[e, j]
            rel = lax.rem(lax.div(a, EY) - strip * row_count + (1 + sheet_rows), sheet_rows)
            places.append(rel * EY + lax.rem(a, EY))
        here = e + EY
        wanted = [
            here, here - EY, here + EY,
            (r + 1) * EY + lax.rem(c + EY - 1, EY), (r + 1) * EY + lax.rem(c + 1, EY),
        ]
        for d in range(5):
            slot = jnp.int32(0)
            for j in range(1, 5):
                slot = slot + jnp.where(places[j] == wanted[d], jnp.int32(j), jnp.int32(0))
            slots[e * 5 + d] = slot
        out = product([ham[e * 5 + j] for j in range(5)], [v0[p] for p in places])
        v1[here] = out.astype(jnp.bfloat16)

    def later_product(ref, r, c):
        e = r * EY + c
        here = e + EY
        line = (r + 1) * EY
        fields = [
            ref[here], ref[here - EY], ref[here + EY],
            ref[line + lax.rem(c + EY - 1, EY)], ref[line + lax.rem(c + 1, EY)],
        ]
        return product([ham[e * 5 + slots[e * 5 + d]] for d in range(5)], fields)

    def second_element(r, c):
        here = r * EY + c + EY
        out = 2.0 * later_product(v1, r, c) - v0[here].astype(jnp.float32)
        v2[here] = out.astype(jnp.bfloat16)

    STEP = 4

    def one_row(element, r):
        def body(g, carry):
            for m in range(STEP):
                element(r, g * STEP + m)
            return carry

        lax.fori_loop(0, EY // STEP, body, 0)

    own_copy.wait()
    for copy in halos[0]:
        copy.wait_recv()
    for r in row_order:
        ham_copies[r].wait()
        one_row(first_element, r)
        if r == 0:
            halos[1][0].start()
        if r == row_count - 1:
            halos[1][1].start()
    for r in row_order:
        if r == 0:
            halos[1][1].wait_recv()
        if r == row_count - 1:
            halos[1][0].wait_recv()
        one_row(second_element, r)
        if r == 0:
            halos[2][0].start()
        if r == row_count - 1:
            halos[2][1].start()
    for copy in halos[2]:
        copy.wait_recv()

    occ = occ_ref[...]

    def density_part(r, c):
        out = 2.0 * later_product(v2, r, c) - v1[r * EY + c + EY].astype(jnp.float32)
        filtered = out.astype(jnp.bfloat16)
        weighted = (filtered.astype(jnp.float32) * occ).astype(jnp.bfloat16)
        return lax.dot_general(
            weighted, filtered, (((1,), (1,)), ((), ())), preferred_element_type=jnp.float32
        )

    def order(o):
        return [(o + t) % bits for t in range(bits)]

    def part_copy(k, s, o, bit):
        return pltpu.make_async_remote_copy(
            packed.at[k, s, o], arrived.at[k, s, o],
            part_send.at[k, s, o], part_recv.at[k, s, o], device_id={"band": partner(bit)},
        )

    def sent_in(o, t):
        seq = order(o)
        return [
            s for s in range(group)
            if s >> seq[t] & 1 and not any(s >> b & 1 for b in seq[:t])
        ]

    def fold(k, t):
        for o in range(pairs):
            bit = order(o)[t]
            for s in sent_in(o, t):
                part_copy(k, s, o, bit).wait_recv()
                kept = s - (1 << bit)
                packed[k, kept, o] = (
                    packed[k, kept, o].astype(jnp.float32) + arrived[k, s, o].astype(jnp.float32)
                ).astype(jnp.bfloat16)
            if t + 1 < bits:
                for s in sent_in(o, t + 1):
                    part_copy(k, s, o, order(o)[t + 1]).start()

    def row_at(k):
        return (my_row + 1 + k) % row_count

    def cross_copy(k):
        return pltpu.make_async_remote_copy(
            packed.at[k, 0], crossed.at[k], cross_send.at[k], cross_recv.at[k],
            device_id={"band": row_at(k) * group + mine},
        )

    for k in range(row_count):
        r = row_at(k)

        def slot_body(i, carry, k=k, r=r):
            s = group - 1 - i
            owner = 0
            for b in range(bits):
                owner = owner + ((s // (1 << b) + mine // (1 << b)) % 2) * (1 << b)
            for o in range(pairs):
                c = owner * owned + 2 * o
                both = pack_pair(density_part(r, c), density_part(r, c + 1))
                packed[k, s, o] = both.astype(jnp.bfloat16)
            for o in range(pairs):
                bit = order(o)[0]

                @pl.when((s // (1 << bit)) % 2 == 1)
                def _():
                    part_copy(k, s, o, bit).start()

            if k > 0:
                @pl.when(i == group // 2 - 1)
                def _():
                    fold(k - 1, 0)

            return carry

        lax.fori_loop(0, group, slot_body, 0)
        if k > 0:
            for t in range(1, bits):
                fold(k - 1, t)
            cross_copy(k - 1).start()

    last = row_count - 1
    for t in range(bits):
        fold(last, t)
    for k in range(last):
        cross_copy(k).wait_recv()
    for o in range(pairs):
        total = packed[last, 0, o].astype(jnp.float32)
        for k in range(last):
            total = total + crossed[k, o].astype(jnp.float32)
        first, second = unpack_pair(total / total_bands)
        out_ref[2 * o] = first
        out_ref[2 * o + 1] = second

    for up, down in halos:
        up.wait_send()
        down.wait_send()
    for k in range(row_count):
        for o in range(pairs):
            for t in range(bits):
                for s in sent_in(o, t):
                    part_copy(k, s, o, order(o)[t]).wait_send()
        if k < last:
            cross_copy(k).wait_send()


def local(strips, bands, coeffs, hamiltonian, adjacency, occupation):
    elems, basis, columns = coeffs.shape
    row_count = elems // EY
    group = bands // row_count
    owned = EY // group
    assert group * row_count == bands and group * owned == EY and group & (group - 1) == 0
    assert owned % 2 == 0 and row_count >= 3 and strips >= 2 and columns == basis
    field = pltpu.VMEM((elems + 2 * EY, basis, columns), jnp.bfloat16)
    block = (owned // 2, basis + PAD, basis)
    dma = pltpu.SemaphoreType.DMA
    flops = 2 * elems * basis * basis * columns * 16
    return pl.pallas_call(
        functools.partial(kernel, strips, bands, float(columns * bands)),
        out_shape=jax.ShapeDtypeStruct((owned, basis, basis), jnp.float32),
        in_specs=[
            pl.BlockSpec(memory_space=pltpu.SMEM),
            pl.BlockSpec(memory_space=pltpu.VMEM),
            pl.BlockSpec(memory_space=pl.ANY),
            pl.BlockSpec(memory_space=pl.ANY),
        ],
        out_specs=pl.BlockSpec(memory_space=pltpu.VMEM),
        scratch_shapes=[
            pltpu.VMEM((elems * 5, basis, basis), jnp.bfloat16),
            field, field, field,
            pltpu.VMEM((row_count, group) + block, jnp.bfloat16),
            pltpu.VMEM((row_count, group) + block, jnp.bfloat16),
            pltpu.VMEM((row_count - 1,) + block, jnp.bfloat16),
            pltpu.SMEM((elems * 5,), jnp.int32),
            dma((row_count,)), dma, dma((6,)), dma((6,)),
            dma((row_count, group, owned // 2)), dma((row_count, group, owned // 2)),
            dma((row_count - 1,)), dma((row_count - 1,)),
        ],
        compiler_params=pltpu.CompilerParams(
            collective_id=0, has_side_effects=True, vmem_limit_bytes=48 * MIB
        ),
        cost_estimate=pl.CostEstimate(
            flops=flops, bytes_accessed=2 * elems * basis * (5 * basis + columns), transcendentals=0
        ),
        name="chebyshev_density",
    )(
        adjacency,
        occupation.reshape(1, columns),
        coeffs,
        hamiltonian.reshape(elems * 5, basis, basis),
    )


def solution(mesh):
    return jax.shard_map(
        functools.partial(local, mesh.shape["strip"], mesh.shape["band"]),
        mesh=mesh,
        in_specs=(
            P("strip", None, "band"),
            P("strip", None, None, None),
            P("strip", None),
            P("band"),
        ),
        out_specs=P(("strip", "band"), None, None),
        check_vma=False,
    )
```

time: 183 us -> 49.9 us (0.27); the launches traced: 181 us -> 49.7 us
  blocking collectives: 68.7 us -> 0 us
  local copies, waits for them, and re-layouts: 62.1 us -> 3.73 us
  Pallas kernels: 0 us -> 46 us
  matrix products: 30.9 us -> 0 us
  starting transfers between devices: 10 us -> 0 us
  other arithmetic: 5.5 us -> 0 us
  waiting for transfers between devices: 3.29 us -> 0 us
    all_gather x1 -> x0, blocking collectives: 68.7 us -> none  [local(): occ_full = lax.all_gather(occupation, 'band', axis=0, tiled=True)]
    gather x4 -> x0, local copies, waits for them, and re-layouts: 46.9 us -> none  [apply_operator(): picked = jnp.take(padded, local_index, axis=0)]
    pallas_call x0 -> x1, Pallas kernels: none -> 46 us  [local(): pl.pallas_call(functools.partial(kernel, strips, bands, float(columns * b...]
    dot_general x4 -> x0, matrix products: 30.9 us -> none  [the longest x3 29.5 us: apply_operator(): jnp.einsum('ejik,ejkb->eib', hamiltonian, picked, preferred_element_type=...]
    all_to_all x1 -> x0, starting transfers between devices: 8.36 us -> none  [local(): lax.all_to_all(grouped, 'band', split_axis=0, concat_axis=3, tiled=True)]
    all_to_all x2 -> x0, local copies, waits for them, and re-layouts: 5.74 us -> none  [local(): lax.all_to_all(grouped, 'band', split_axis=0, concat_axis=3, tiled=True)]
    concatenate x3 -> x0, other arithmetic: 4.78 us -> none  [with_halo(): block = jnp.concatenate([low, block, high], axis=dim)]
    ppermute x6 -> x0, waiting for transfers between devices: 3.29 us -> none  [the longest x3 1.79 us: with_halo(): lax.ppermute(lax.slice_in_dim(block, block.shape[dim] - width, None, axis...]
  transfers between devices with their start and end apart: 7 -> 0, of which waited for: 4 -> 0; matrix products, arithmetic and copies ran while one was open for 2% -> 0% of each run, Pallas kernels for 0% -> 0%
where the time goes in v1:
time: 49.9 us; the launch traced here: 49.7 us
  Pallas kernels  46 us (92%)
  local copies, waits for them, and re-layouts  3.73 us (7%)
    pallas_call x1, Pallas kernels, local(): pl.pallas_call(functools.partial(kernel, strips, bands, float(columns * b...  46 us
    unnamed x6, local copies, waits for them, and re-layouts  3.73 us

profile of v1, /device:TPU:0, one launch (start us, length us, event | category | flops | bytes accessed | tf_op | source)
XLA Modules:
  0.0 49.7 jit_solution(11305445428147416048)
XLA Ops:
  0.0 0.8 %copy.5.adj_ref = s32[64,5]{1,0:T(8,128)S(1)} copy(s32[64,5]{0,1:T(8,128)} %param.6) | data formatting | bytes 2560 | tf_op args[2]
  0.8 0.0 copy-start
  0.8 1.6 %copy-done = bf16[64,128,128]{2,1,0:T(8,128)(2,1)S(1)} copy-done((bf16[64,128,128]{2,1,0:T(8,128)(2,1)S(1)}, bf16[64,128,128]{2,1,0:T(8,128)(2,1)}, u32[]{:S(2)}) %copy-start) | copy-done | bytes 2097176
  2.4 0.0 copy-start.1
  2.4 0.7 %copy-done.1 = f32[128]{0:T(128)S(1)} copy-done((f32[128]{0:T(128)S(1)}, f32[128]{0:T(128)}, u32[]{:S(2)}) %copy-start.1) | copy-done | bytes 536
  3.0 46.0 %chebyshev_density.1 = f32[4,128,128]{2,1,0:T(8,128)S(1)} custom-call(s32[64,5]{1,0:T(8,128)S(1)} %copy.5.adj_ref, f32[1,128]{1,0:T(1,128)S(1)} %bitcast.2, bf16[64,128,128]{2,1,0:T(8,128)(2,1)S(1)} %copy-done, bf16[320,128,128]{2,1,0:T(8,128)(2,1)} %bitcast.3), custom_call_target="tpu_custom_call" | custom-call | flops 4294967296 | bytes 12582912 | tf_op jit(solution)/shard_map/chebyshev_density/pallas_call | solution.py:310
  49.0 0.7 %copy.7 = f32[4,128,128]{2,1,0:T(8,128)} copy(f32[4,128,128]{2,1,0:T(8,128)S(1)} %chebyshev_density.1) | data formatting | bytes 524288
Async XLA Ops:
  0.8 1.6 %copy-start = (bf16[64,128,128]{2,1,0:T(8,128)(2,1)S(1)}, bf16[64,128,128]{2,1,0:T(8,128)(2,1)}, u32[]{:S(2)}) copy-start(bf16[64,128,128]{2,1,0:T(8,128)(2,1)} %coeffs_hbm.1) | copy-start | bytes 6291460
  2.4 0.7 %copy-start.1 = (f32[128]{0:T(128)S(1)}, f32[128]{0:T(128)}, u32[]{:S(2)}) copy-start(f32[128]{0:T(128)} %param.7) | copy-start | bytes 1540

commit v2 on v1

--- a/solution.py
+++ b/solution.py
@@ -53,9 +53,9 @@
 
 def kernel(
     strips, bands, total_bands,
-    adj_ref, occ_ref, coeffs_hbm, ham_hbm, out_ref,
-    ham, v0, v1, v2, packed, arrived, crossed, slots,
-    ham_sem, v0_sem, halo_send, halo_recv, part_send, part_recv, cross_send, cross_recv,
+    adj_hbm, occ_hbm, coeffs_hbm, ham_hbm, out_ref,
+    ham, v0, v0_first, v0_last, v1, v2, packed, arrived, crossed, adj_ref, occ_ref, table, slots,
+    ham_sem, own_sem, halo_send, halo_recv, part_send, part_recv, cross_send, cross_recv,
 ):
     elems = coeffs_hbm.shape[0]
     row_count = elems // EY
@@ -72,7 +72,11 @@
         step = 1 << bit
         return band + step * (1 - 2 * ((band // step) % 2))
 
-    own_copy = pltpu.make_async_copy(coeffs_hbm, v0.at[pl.ds(EY, elems)], v0_sem)
+    adj_copy = pltpu.make_async_copy(adj_hbm, adj_ref, own_sem.at[0])
+    occ_copy = pltpu.make_async_copy(occ_hbm, occ_ref, own_sem.at[1])
+    own_copy = pltpu.make_async_copy(coeffs_hbm, v0, own_sem.at[2])
+    table_copy = pltpu.make_async_copy(table, slots, own_sem.at[3])
+    adj_copy.start()
     own_copy.start()
     per_row = EY * 5
     ham_copies = [
@@ -81,9 +85,12 @@
         )
         for r in range(row_count)
     ]
-    row_order = [1, 0] + [row_count - 1] + list(range(2, row_count - 1))
-    for r in row_order:
+    last = row_count - 1
+    first_order = list(range(1, last)) + [0, last]
+    row_order = [1, 0, last] + list(range(2, last))
+    for r in first_order:
         ham_copies[r].start()
+    occ_copy.start()
 
     barrier = pltpu.get_barrier_semaphore()
     greeted = 0
@@ -98,20 +105,44 @@
             barrier, inc=1, device_id={"band": ((my_row + away) % row_count) * group + mine}
         )
         greeted += 1
+
+    adj_copy.wait()
+    sheet_rows = row_count * strips
+    a = adj_ref[...]
+    places = lax.rem(lax.div(a, EY) - strip * row_count + sheet_rows, sheet_rows) * EY + lax.rem(a, EY)
+    here = lanes((1, elems))
+    line, col = lax.div(here, EY), lax.rem(here, EY)
+    wanted = [
+        here,
+        lax.rem(line + sheet_rows - 1, sheet_rows) * EY + col,
+        lax.rem(line + 1, sheet_rows) * EY + col,
+        line * EY + lax.rem(col + EY - 1, EY),
+        line * EY + lax.rem(col + 1, EY),
+    ]
+    for d in range(5):
+        slot = here * 0
+        for j in range(1, 5):
+            slot = slot + jnp.where(places[j:j + 1] == wanted[d], j, 0)
+        table[d:d + 1, :elems] = jnp.minimum(slot, 4)
+        table[8 + d:9 + d, :elems] = jnp.minimum(places[d:d + 1], elems - 1)
+    table_copy.start()
     pl.semaphore_wait(barrier, greeted)
 
-    def halo(field, ref, source, shift):
+    def halo(field, source, shift, first, final):
         up = pltpu.make_async_remote_copy(
-            source.at[pl.ds(shift, EY)], ref.at[pl.ds(EY + elems, EY)],
+            source.at[pl.ds(shift, EY)], final,
             halo_send.at[2 * field], halo_recv.at[2 * field], device_id={"strip": above},
         )
         down = pltpu.make_async_remote_copy(
-            source.at[pl.ds(shift + elems - EY, EY)], ref.at[pl.ds(0, EY)],
+            source.at[pl.ds(shift + elems - EY, EY)], first,
             halo_send.at[2 * field + 1], halo_recv.at[2 * field + 1], device_id={"strip": below},
         )
         return up, down
 
-    halos = [halo(0, v0, coeffs_hbm, 0), halo(1, v1, v1, EY), halo(2, v2, v2, EY)]
+    ends = [(v.at[pl.ds(0, EY)], v.at[pl.ds(EY + elems, EY)]) for v in (v1, v2)]
+    halos = [
+        halo(0, coeffs_hbm, 0, v0_first, v0_last), halo(1, v1, EY, *ends[0]), halo(2, v2, EY, *ends[1])
+    ]
     for copy in halos[0]:
         copy.start()
 
@@ -121,27 +152,26 @@
             preferred_element_type=jnp.float32,
         )
 
-    sheet_rows = row_count * strips
-
-    def first_element(r, c):
+    def inner_element(r, c):
         e = r * EY + c
-        places = []
-        for j in range(5):
-            a = adj_ref[e, j]
-            rel = lax.rem(lax.div(a, EY) - strip * row_count + (1 + sheet_rows), sheet_rows)
-            places.append(rel * EY + lax.rem(a, EY))
-        here = e + EY
-        wanted = [
-            here, here - EY, here + EY,
-            (r + 1) * EY + lax.rem(c + EY - 1, EY), (r + 1) * EY + lax.rem(c + 1, EY),
+        out = product(
+            [ham[e * 5 + j] for j in range(5)], [v0[slots[8 + j, e]] for j in range(5)]
+        )
+        v1[e + EY] = out.astype(jnp.bfloat16)
+
+    def blocks_of(e):
+        return [ham[e * 5 + slots[d, e]] for d in range(5)]
+
+    def outer_element(r, c):
+        e = r * EY + c
+        line = r * EY
+        fields = [
+            v0[e],
+            v0_first[c] if r == 0 else v0[e - EY],
+            v0_last[c] if r == last else v0[e + EY],
+            v0[line + lax.rem(c + EY - 1, EY)], v0[line + lax.rem(c + 1, EY)],
         ]
-        for d in range(5):
-            slot = jnp.int32(0)
-            for j in range(1, 5):
-                slot = slot + jnp.where(places[j] == wanted[d], jnp.int32(j), jnp.int32(0))
-            slots[e * 5 + d] = slot
-        out = product([ham[e * 5 + j] for j in range(5)], [v0[p] for p in places])
-        v1[here] = out.astype(jnp.bfloat16)
+        v1[e + EY] = product(blocks_of(e), fields).astype(jnp.bfloat16)
 
     def later_product(ref, r, c):
         e = r * EY + c
@@ -151,12 +181,12 @@
             ref[here], ref[here - EY], ref[here + EY],
             ref[line + lax.rem(c + EY - 1, EY)], ref[line + lax.rem(c + 1, EY)],
         ]
-        return product([ham[e * 5 + slots[e * 5 + d]] for d in range(5)], fields)
+        return product(blocks_of(e), fields)
 
     def second_element(r, c):
-        here = r * EY + c + EY
-        out = 2.0 * later_product(v1, r, c) - v0[here].astype(jnp.float32)
-        v2[here] = out.astype(jnp.bfloat16)
+        e = r * EY + c
+        out = 2.0 * later_product(v1, r, c) - v0[e].astype(jnp.float32)
+        v2[e + EY] = out.astype(jnp.bfloat16)
 
     STEP = 4
 
@@ -169,11 +199,16 @@
         lax.fori_loop(0, EY // STEP, body, 0)
 
     own_copy.wait()
+    table_copy.wait()
+    for r in first_order[:-2]:
+        ham_copies[r].wait()
+        one_row(inner_element, r)
+    for r in (0, last):
+        ham_copies[r].wait()
     for copy in halos[0]:
         copy.wait_recv()
-    for r in row_order:
-        ham_copies[r].wait()
-        one_row(first_element, r)
+    for r in (0, last):
+        one_row(outer_element, r)
         if r == 0:
             halos[1][0].start()
         if r == row_count - 1:
@@ -191,6 +226,7 @@
     for copy in halos[2]:
         copy.wait_recv()
 
+    occ_copy.wait()
     occ = occ_ref[...]
 
     def density_part(r, c):
@@ -271,7 +307,6 @@
                 fold(k - 1, t)
             cross_copy(k - 1).start()
 
-    last = row_count - 1
     for t in range(bits):
         fold(last, t)
     for k in range(last):
@@ -303,40 +338,46 @@
     owned = EY // group
     assert group * row_count == bands and group * owned == EY and group & (group - 1) == 0
     assert owned % 2 == 0 and row_count >= 3 and strips >= 2 and columns == basis
+    edge = pltpu.VMEM((EY, basis, columns), jnp.bfloat16)
+    own = pltpu.VMEM((elems, basis, columns), jnp.bfloat16)
     field = pltpu.VMEM((elems + 2 * EY, basis, columns), jnp.bfloat16)
     block = (owned // 2, basis + PAD, basis)
+    wide = -(-elems // 128) * 128
     dma = pltpu.SemaphoreType.DMA
     flops = 2 * elems * basis * basis * columns * 16
     return pl.pallas_call(
         functools.partial(kernel, strips, bands, float(columns * bands)),
         out_shape=jax.ShapeDtypeStruct((owned, basis, basis), jnp.float32),
         in_specs=[
-            pl.BlockSpec(memory_space=pltpu.SMEM),
-            pl.BlockSpec(memory_space=pltpu.VMEM),
+            pl.BlockSpec(memory_space=pl.ANY),
+            pl.BlockSpec(memory_space=pl.ANY),
             pl.BlockSpec(memory_space=pl.ANY),
             pl.BlockSpec(memory_space=pl.ANY),
         ],
         out_specs=pl.BlockSpec(memory_space=pltpu.VMEM),
         scratch_shapes=[
             pltpu.VMEM((elems * 5, basis, basis), jnp.bfloat16),
-            field, field, field,
+            own, edge, edge, field, field,
             pltpu.VMEM((row_count, group) + block, jnp.bfloat16),
             pltpu.VMEM((row_count, group) + block, jnp.bfloat16),
             pltpu.VMEM((row_count - 1,) + block, jnp.bfloat16),
-            pltpu.SMEM((elems * 5,), jnp.int32),
-            dma((row_count,)), dma, dma((6,)), dma((6,)),
+            pltpu.VMEM((5, elems), jnp.int32),
+            pltpu.VMEM((1, columns), jnp.float32),
+            pltpu.VMEM((16, wide), jnp.int32),
+            pltpu.SMEM((16, wide), jnp.int32),
+            dma((row_count,)), dma((4,)), dma((6,)), dma((6,)),
             dma((row_count, group, owned // 2)), dma((row_count, group, owned // 2)),
             dma((row_count - 1,)), dma((row_count - 1,)),
         ],
         compiler_params=pltpu.CompilerParams(
-            collective_id=0, has_side_effects=True, vmem_limit_bytes=48 * MIB
+            collective_id=0, has_side_effects=True, vmem_limit_bytes=63 * MIB
         ),
         cost_estimate=pl.CostEstimate(
             flops=flops, bytes_accessed=2 * elems * basis * (5 * basis + columns), transcendentals=0
         ),
         name="chebyshev_density",
     )(
-        adjacency,
+        adjacency.T,
         occupation.reshape(1, columns),
         coeffs,
         hamiltonian.reshape(elems * 5, basis, basis),

time: 49.9 us -> 44 us (0.88)
  Pallas kernels: 46 us -> 42.1 us
  local copies, waits for them, and re-layouts: 3.73 us -> 1.67 us
    pallas_call x1, Pallas kernels: 46 us -> 42.1 us  [local(): pl.pallas_call(functools.partial(kernel, strips, bands, float(columns * b...]
    unnamed x6 -> x1, local copies, waits for them, and re-layouts: 3.73 us -> 1.67 us
where the time goes in v2:
time: 44 us; the launch traced here: 43.8 us
  Pallas kernels  42.1 us (96%)
  local copies, waits for them, and re-layouts  1.67 us (4%)
    pallas_call x1, Pallas kernels, local(): pl.pallas_call(functools.partial(kernel, strips, bands, float(columns * b...  42.1 us
    unnamed x1, local copies, waits for them, and re-layouts  1.67 us

profile of v2, /device:TPU:0, one launch (start us, length us, event | category | flops | bytes accessed | tf_op | source)
XLA Modules:
  0.0 43.8 jit_solution(1639754685596073302)
XLA Ops:
  0.0 42.1 %chebyshev_density.1 = f32[4,128,128]{2,1,0:T(8,128)} custom-call(s32[5,64]{1,0:T(8,128)} %bitcast.4, f32[1,128]{1,0:T(1,128)} %bitcast.5, bf16[64,128,128]{2,1,0:T(8,128)(2,1)} %coeffs_hbm.1, bf16[320,128,128]{2,1,0:T(8,128)(2,1)} %bitcast.3), custom_call_target="tpu_custom_call" | custom-call | flops 4294967296 | bytes 12582912 | tf_op jit(solution)/shard_map/chebyshev_density/pallas_call | solution.py:348
  42.2 1.7 %copy.6 = f32[4,128,128]{2,1,0:T(8,128)} copy(f32[4,128,128]{2,1,0:T(8,128)} %chebyshev_density.1) | data formatting | bytes 524288

commit v3 on v2

--- a/solution.py
+++ b/solution.py
@@ -188,7 +188,7 @@
         out = 2.0 * later_product(v1, r, c) - v0[e].astype(jnp.float32)
         v2[e + EY] = out.astype(jnp.bfloat16)
 
-    STEP = 4
+    STEP = 16
 
     def one_row(element, r):
         def body(g, carry):
@@ -278,7 +278,7 @@
     for k in range(row_count):
         r = row_at(k)
 
-        def slot_body(i, carry, k=k, r=r):
+        for i in range(group):
             s = group - 1 - i
             owner = 0
             for b in range(bits):
@@ -288,20 +288,10 @@
                 both = pack_pair(density_part(r, c), density_part(r, c + 1))
                 packed[k, s, o] = both.astype(jnp.bfloat16)
             for o in range(pairs):
-                bit = order(o)[0]
-
-                @pl.when((s // (1 << bit)) % 2 == 1)
-                def _():
-                    part_copy(k, s, o, bit).start()
-
-            if k > 0:
-                @pl.when(i == group // 2 - 1)
-                def _():
-                    fold(k - 1, 0)
-
-            return carry
-
-        lax.fori_loop(0, group, slot_body, 0)
+                if s in sent_in(o, 0):
+                    part_copy(k, s, o, order(o)[0]).start()
+            if k > 0 and i == group // 2 - 1:
+                fold(k - 1, 0)
         if k > 0:
             for t in range(1, bits):
                 fold(k - 1, t)
@@ -370,7 +360,7 @@
             dma((row_count - 1,)), dma((row_count - 1,)),
         ],
         compiler_params=pltpu.CompilerParams(
-            collective_id=0, has_side_effects=True, vmem_limit_bytes=63 * MIB
+            collective_id=0, has_side_effects=True, vmem_limit_bytes=62 * MIB
         ),
         cost_estimate=pl.CostEstimate(
             flops=flops, bytes_accessed=2 * elems * basis * (5 * basis + columns), transcendentals=0

time: 44 us -> 41.3 us (0.939)
  Pallas kernels: 42.1 us -> 39.4 us
    pallas_call x1, Pallas kernels: 42.1 us -> 39.4 us  [local(): pl.pallas_call(functools.partial(kernel, strips, bands, float(columns * b...]
where the time goes in v3:
time: 41.3 us; the launch traced here: 41.1 us
  Pallas kernels  39.4 us (95%)
  local copies, waits for them, and re-layouts  1.67 us (4%)
    pallas_call x1, Pallas kernels, local(): pl.pallas_call(functools.partial(kernel, strips, bands, float(columns * b...  39.4 us
    unnamed x1, local copies, waits for them, and re-layouts  1.67 us

profile of v3, /device:TPU:0, one launch (start us, length us, event | category | flops | bytes accessed | tf_op | source)
XLA Modules:
  0.0 41.1 jit_solution(9236969582252122510)
XLA Ops:
  0.0 39.4 %chebyshev_density.1 = f32[4,128,128]{2,1,0:T(8,128)} custom-call(s32[5,64]{1,0:T(8,128)} %bitcast.4, f32[1,128]{1,0:T(1,128)} %bitcast.5, bf16[64,128,128]{2,1,0:T(8,128)(2,1)} %coeffs_hbm.1, bf16[320,128,128]{2,1,0:T(8,128)(2,1)} %bitcast.3), custom_call_target="tpu_custom_call" | custom-call | flops 4294967296 | bytes 12582912 | tf_op jit(solution)/shard_map/chebyshev_density/pallas_call | solution.py:338
  39.5 1.7 %copy.6 = f32[4,128,128]{2,1,0:T(8,128)} copy(f32[4,128,128]{2,1,0:T(8,128)} %chebyshev_density.1) | data formatting | bytes 524288

commit v4 on v3

--- a/solution.py
+++ b/solution.py
@@ -162,53 +162,63 @@
     def blocks_of(e):
         return [ham[e * 5 + slots[d, e]] for d in range(5)]
 
-    def outer_element(r, c):
+    def pair_product(e, field, above_of, below_of, line, c):
+        first, second = blocks_of(e), blocks_of(e + 1)
+        between = product(
+            [
+                jnp.concatenate([first[0], second[3]], axis=0),
+                jnp.concatenate([first[4], second[0]], axis=0),
+            ],
+            [field[line + c], field[line + c + 1]],
+        )
+        rest_1 = product(
+            first[1:4], [above_of(c), below_of(c), field[line + lax.rem(c + EY - 1, EY)]]
+        )
+        rest_2 = product(
+            [second[1], second[2], second[4]],
+            [above_of(c + 1), below_of(c + 1), field[line + lax.rem(c + 2, EY)]],
+        )
+        return between[:rest_1.shape[0]] + rest_1, between[rest_1.shape[0]:] + rest_2
+
+    def outer_pair(r, c):
+        line = r * EY
+        pair = pair_product(
+            line + c, v0,
+            lambda at: v0_first[at] if r == 0 else v0[line - EY + at],
+            lambda at: v0_last[at] if r == last else v0[line + EY + at],
+            line, c,
+        )
+        for m in range(2):
+            v1[line + c + m + EY] = pair[m].astype(jnp.bfloat16)
+
+    def later_pair(ref, r, c):
+        line = (r + 1) * EY
+        return pair_product(
+            r * EY + c, ref, lambda at: ref[line - EY + at], lambda at: ref[line + EY + at], line, c
+        )
+
+    def second_pair(r, c):
         e = r * EY + c
-        line = r * EY
-        fields = [
-            v0[e],
-            v0_first[c] if r == 0 else v0[e - EY],
-            v0_last[c] if r == last else v0[e + EY],
-            v0[line + lax.rem(c + EY - 1, EY)], v0[line + lax.rem(c + 1, EY)],
-        ]
-        v1[e + EY] = product(blocks_of(e), fields).astype(jnp.bfloat16)
-
-    def later_product(ref, r, c):
-        e = r * EY + c
-        here = e + EY
-        line = (r + 1) * EY
-        fields = [
-            ref[here], ref[here - EY], ref[here + EY],
-            ref[line + lax.rem(c + EY - 1, EY)], ref[line + lax.rem(c + 1, EY)],
-        ]
-        return product(blocks_of(e), fields)
-
-    def second_element(r, c):
-        e = r * EY + c
-        out = 2.0 * later_product(v1, r, c) - v0[e].astype(jnp.float32)
-        v2[e + EY] = out.astype(jnp.bfloat16)
-
-    STEP = 16
-
-    def one_row(element, r):
-        def body(g, carry):
-            for m in range(STEP):
-                element(r, g * STEP + m)
-            return carry
-
-        lax.fori_loop(0, EY // STEP, body, 0)
+        pair = later_pair(v1, r, c)
+        for m in range(2):
+            out = 2.0 * pair[m] - v0[e + m].astype(jnp.float32)
+            v2[e + m + EY] = out.astype(jnp.bfloat16)
+
+    def one_row(step, element, r):
+        for c in range(0, EY, step):
+            element(r, c)
 
     own_copy.wait()
     table_copy.wait()
     for r in first_order[:-2]:
         ham_copies[r].wait()
-        one_row(inner_element, r)
+        one_row(1, inner_element, r)
     for r in (0, last):
         ham_copies[r].wait()
     for copy in halos[0]:
         copy.wait_recv()
     for r in (0, last):
-        one_row(outer_element, r)
+        one_row(2, outer_pair, r)
         if r == 0:
             halos[1][0].start()
         if r == row_count - 1:
@@ -218,7 +228,7 @@
             halos[1][1].wait_recv()
         if r == row_count - 1:
             halos[1][0].wait_recv()
-        one_row(second_element, r)
+        one_row(2, second_pair, r)
         if r == 0:
             halos[2][0].start()
         if r == row_count - 1:
@@ -229,13 +239,16 @@
     occ_copy.wait()
     occ = occ_ref[...]
 
-    def density_part(r, c):
-        out = 2.0 * later_product(v2, r, c) - v1[r * EY + c + EY].astype(jnp.float32)
-        filtered = out.astype(jnp.bfloat16)
-        weighted = (filtered.astype(jnp.float32) * occ).astype(jnp.bfloat16)
-        return lax.dot_general(
-            weighted, filtered, (((1,), (1,)), ((), ())), preferred_element_type=jnp.float32
-        )
+    def density_pair(r, c):
+        parts = []
+        for m, product_m in enumerate(later_pair(v2, r, c)):
+            out = 2.0 * product_m - v1[r * EY + c + m + EY].astype(jnp.float32)
+            filtered = out.astype(jnp.bfloat16)
+            weighted = (filtered.astype(jnp.float32) * occ).astype(jnp.bfloat16)
+            parts.append(lax.dot_general(
+                weighted, filtered, (((1,), (1,)), ((), ())), preferred_element_type=jnp.float32
+            ))
+        return parts
 
     def order(o):
         return [(o + t) % bits for t in range(bits)]
@@ -285,7 +298,7 @@
                 owner = owner + ((s // (1 << b) + mine // (1 << b)) % 2) * (1 << b)
             for o in range(pairs):
                 c = owner * owned + 2 * o
-                both = pack_pair(density_part(r, c), density_part(r, c + 1))
+                both = pack_pair(*density_pair(r, c))
                 packed[k, s, o] = both.astype(jnp.bfloat16)
             for o in range(pairs):
                 if s in sent_in(o, 0):

time: 41.3 us -> 39.2 us (0.949)
  Pallas kernels: 39.4 us -> 37.4 us
    pallas_call x1, Pallas kernels: 39.4 us -> 37.4 us  [local(): pl.pallas_call(functools.partial(kernel, strips, bands, float(columns * b...]
where the time goes in v4:
time: 39.2 us; the launch traced here: 39.1 us
  Pallas kernels  37.4 us (95%)
  local copies, waits for them, and re-layouts  1.67 us (4%)
    pallas_call x1, Pallas kernels, local(): pl.pallas_call(functools.partial(kernel, strips, bands, float(columns * b...  37.4 us
    unnamed x1, local copies, waits for them, and re-layouts  1.67 us

profile of v4, /device:TPU:0, one launch (start us, length us, event | category | flops | bytes accessed | tf_op | source)
XLA Modules:
  0.0 39.1 jit_solution(12696225514676365026)
XLA Ops:
  0.0 37.4 %chebyshev_density.1 = f32[4,128,128]{2,1,0:T(8,128)} custom-call(s32[5,64]{1,0:T(8,128)} %bitcast.4, f32[1,128]{1,0:T(1,128)} %bitcast.5, bf16[64,128,128]{2,1,0:T(8,128)(2,1)} %coeffs_hbm.1, bf16[320,128,128]{2,1,0:T(8,128)(2,1)} %bitcast.3), custom_call_target="tpu_custom_call" | custom-call | flops 4294967296 | bytes 12582912 | tf_op jit(solution)/shard_map/chebyshev_density/pallas_call | solution.py:351
  37.4 1.7 %copy.6 = f32[4,128,128]{2,1,0:T(8,128)} copy(f32[4,128,128]{2,1,0:T(8,128)} %chebyshev_density.1) | data formatting | bytes 524288

commit v5 on v4

--- a/solution.py
+++ b/solution.py
@@ -266,18 +266,21 @@
             if s >> seq[t] & 1 and not any(s >> b & 1 for b in seq[:t])
         ]
 
-    def fold(k, t):
-        for o in range(pairs):
-            bit = order(o)[t]
-            for s in sent_in(o, t):
-                part_copy(k, s, o, bit).wait_recv()
-                kept = s - (1 << bit)
-                packed[k, kept, o] = (
-                    packed[k, kept, o].astype(jnp.float32) + arrived[k, s, o].astype(jnp.float32)
-                ).astype(jnp.bfloat16)
-            if t + 1 < bits:
-                for s in sent_in(o, t + 1):
-                    part_copy(k, s, o, order(o)[t + 1]).start()
+    def fold(k, t, passed_on=True, own=True):
+        for keep_own in [False] * passed_on + [True] * own:
+            for o in range(pairs):
+                bit = order(o)[t]
+                for s in sent_in(o, t):
+                    kept = s - (1 << bit)
+                    if (kept == 0) != keep_own:
+                        continue
+                    part_copy(k, s, o, bit).wait_recv()
+                    packed[k, kept, o] = (
+                        packed[k, kept, o].astype(jnp.float32) + arrived[k, s, o].astype(jnp.float32)
+                    ).astype(jnp.bfloat16)
+                if t + 1 < bits and not keep_own:
+                    for s in sent_in(o, t + 1):
+                        part_copy(k, s, o, order(o)[t + 1]).start()
 
     def row_at(k):
         return (my_row + 1 + k) % row_count
@@ -305,12 +308,15 @@
                     part_copy(k, s, o, order(o)[0]).start()
             if k > 0 and i == group // 2 - 1:
                 fold(k - 1, 0)
-        if k > 0:
-            for t in range(1, bits):
-                fold(k - 1, t)
-            cross_copy(k - 1).start()
-
-    for t in range(bits):
+            if k > 0 and i == group - 2:
+                for t in range(1, bits):
+                    fold(k - 1, t)
+                cross_copy(k - 1).start()
+                if k == last:
+                    fold(last, 0, own=False)
+
+    fold(last, 0, passed_on=False)
+    for t in range(1, bits):
         fold(last, t)
     for k in range(last):
         cross_copy(k).wait_recv()

time: 39.2 us -> 40.1 us (1.023)
  Pallas kernels: 37.4 us -> 38.3 us
    pallas_call x1, Pallas kernels: 37.4 us -> 38.3 us  [local(): pl.pallas_call(functools.partial(kernel, strips, bands, float(columns * b...]
where the time goes in v5:
time: 40.1 us; the launch traced here: 39.9 us
  Pallas kernels  38.3 us (96%)
  local copies, waits for them, and re-layouts  1.67 us (4%)
    pallas_call x1, Pallas kernels, local(): pl.pallas_call(functools.partial(kernel, strips, bands, float(columns * b...  38.3 us
    unnamed x1, local copies, waits for them, and re-layouts  1.67 us

profile of v5, /device:TPU:0, one launch (start us, length us, event | category | flops | bytes accessed | tf_op | source)
XLA Modules:
  0.0 39.9 jit_solution(17652010238739754686)
XLA Ops:
  0.0 38.3 %chebyshev_density.1 = f32[4,128,128]{2,1,0:T(8,128)} custom-call(s32[5,64]{1,0:T(8,128)} %bitcast.4, f32[1,128]{1,0:T(1,128)} %bitcast.5, bf16[64,128,128]{2,1,0:T(8,128)(2,1)} %coeffs_hbm.1, bf16[320,128,128]{2,1,0:T(8,128)(2,1)} %bitcast.3), custom_call_target="tpu_custom_call" | custom-call | flops 4294967296 | bytes 12582912 | tf_op jit(solution)/shard_map/chebyshev_density/pallas_call | solution.py:357
  38.3 1.7 %copy.6 = f32[4,128,128]{2,1,0:T(8,128)} copy(f32[4,128,128]{2,1,0:T(8,128)} %chebyshev_density.1) | data formatting | bytes 524288

commit v6 on v4

--- a/solution.py
+++ b/solution.py
@@ -288,6 +288,11 @@
             device_id={"band": row_at(k) * group + mine},
         )
 
+    def pass_on(k):
+        for t in range(1, bits):
+            fold(k, t)
+        cross_copy(k).start()
+
     for k in range(row_count):
         r = row_at(k)
 
@@ -303,13 +308,12 @@
             for o in range(pairs):
                 if s in sent_in(o, 0):
                     part_copy(k, s, o, order(o)[0]).start()
-            if k > 0 and i == group // 2 - 1:
-                fold(k - 1, 0)
+            if k > 1 and i == group // 2 - 1:
+                pass_on(k - 2)
         if k > 0:
-            for t in range(1, bits):
-                fold(k - 1, t)
-            cross_copy(k - 1).start()
-
+            fold(k - 1, 0)
+
+    pass_on(last - 1)
     for t in range(bits):
         fold(last, t)
     for k in range(last):

time: 39.2 us -> 38.7 us (0.987)
  Pallas kernels: 37.4 us -> 36.9 us
    pallas_call x1, Pallas kernels: 37.4 us -> 36.9 us  [local(): pl.pallas_call(functools.partial(kernel, strips, bands, float(columns * b...]
where the time goes in v6:
time: 38.7 us; the launch traced here: 38.6 us
  Pallas kernels  36.9 us (95%)
  local copies, waits for them, and re-layouts  1.67 us (4%)
    pallas_call x1, Pallas kernels, local(): pl.pallas_call(functools.partial(kernel, strips, bands, float(columns * b...  36.9 us
    unnamed x1, local copies, waits for them, and re-layouts  1.67 us

profile of v6, /device:TPU:0, one launch (start us, length us, event | category | flops | bytes accessed | tf_op | source)
XLA Modules:
  0.0 38.6 jit_solution(14616433339867550053)
XLA Ops:
  0.0 36.9 %chebyshev_density.1 = f32[4,128,128]{2,1,0:T(8,128)} custom-call(s32[5,64]{1,0:T(8,128)} %bitcast.4, f32[1,128]{1,0:T(1,128)} %bitcast.5, bf16[64,128,128]{2,1,0:T(8,128)(2,1)} %coeffs_hbm.1, bf16[320,128,128]{2,1,0:T(8,128)(2,1)} %bitcast.3), custom_call_target="tpu_custom_call" | custom-call | flops 4294967296 | bytes 12582912 | tf_op jit(solution)/shard_map/chebyshev_density/pallas_call | solution.py:355
  36.9 1.7 %copy.6 = f32[4,128,128]{2,1,0:T(8,128)} copy(f32[4,128,128]{2,1,0:T(8,128)} %chebyshev_density.1) | data formatting | bytes 524288
